TPU v7x, 128 devices: a whole 4x4x4 slice. The times are simulated.
128 devices in a mesh: section: 2 (over y_hi), ctx: 4 (over z), dp: 8 (over x, core), tp: 2 (over y_lo).
Axes of the slice: x: 4, y: 4 (y_hi: 2, y_lo: 2; y = y_hi * 2 + y_lo), z: 4, core: 2. Of those that a mesh axis runs over, the one named last changes fastest.
Arguments:
- tokens: bfloat16 [8, 2, 512, 1280], P('dp', None, 'ctx'), may hold values from -6 to 6
- ln_gain: float32 [2, 2, 1280], P('section'), may hold values from 0.25 to 1.75
- ln_bias: float32 [2, 2, 1280], P('section'), may hold values from -1.5 to 1.5
- w_qkv: bfloat16 [2, 1280, 3, 1280], P('section', ('ctx', 'dp'), None, 'tp'), may hold values from -0.15625 to 0.15625
- qv_bias: float32 [2, 2, 1280], P('section', None, 'tp'), may hold values from -1.5 to 1.5
- w_out: bfloat16 [2, 1280, 1280], P('section', 'tp', ('ctx', 'dp')), may hold values from -1 to 1
- branch_bias: float32 [2, 2, 1280], P('section'), may hold values from -1.5 to 1.5
- w_up: bfloat16 [2, 1280, 5120], P('section', ('ctx', 'dp'), 'tp'), may hold values from -0.15625 to 0.15625
- up_bias: float32 [2, 5120], P('section', 'tp'), may hold values from -1.5 to 1.5
- w_down: bfloat16 [2, 5120, 1280], P('section', 'tp', ('ctx', 'dp')), may hold values from -0.078125 to 0.078125
- out_grad: bfloat16 [8, 2, 512, 1280], P('dp', None, 'ctx'), may hold values from -6 to 6
Outputs:
- block_out: bfloat16 [8, 2, 512, 1280], P('dp', 'section', 'ctx')
- tokens_grad: bfloat16 [8, 2, 512, 1280], P('dp', 'section', 'ctx')
- ln_gain_grad: float32 [2, 2, 1280], P('section')
- ln_bias_grad: float32 [2, 2, 1280], P('section')
- w_qkv_grad: float32 [2, 1280, 3, 1280], P('section', ('ctx', 'dp'), None, 'tp')
- qv_bias_grad: float32 [2, 2, 1280], P('section', None, 'tp')
- w_out_grad: float32 [2, 1280, 1280], P('section', 'tp', ('ctx', 'dp'))
- branch_bias_grad: float32 [2, 2, 1280], P('section')
- w_up_grad: float32 [2, 1280, 5120], P('section', ('ctx', 'dp'), 'tp')
- up_bias_grad: float32 [2, 5120], P('section', 'tp')
- w_down_grad: float32 [2, 5120, 1280], P('section', 'tp', ('ctx', 'dp'))
All inputs are finite; a program needn't handle non-finite values.
Results may differ from a plain program's by a relative error of at most 0.02.
Values may be sent and summed in bfloat16 or wider, within the bound.
A program may use at most 192 MiB of HBM per device.

v0:
```python
import jax
import jax.numpy as jnp
from jax import lax
from jax.sharding import PartitionSpec as P

HEAD = 64


EPS = 1e-05
NEG = -1e30
FULL_PRECISION = lax.Precision.HIGHEST


def from_behind(shard, axis, by):
    length = lax.axis_size(axis)
    return lax.ppermute(shard, axis, [(i, (i + by) % length) for i in range(length)])


def passed_along(value, axis, steps):
    count = lax.axis_size(axis)
    initial, last = (max(0, -steps), min(count, count - steps))
    return lax.ppermute(value, axis, [(source, source + steps) for source in range(initial, last)])


def norm_forward(rows_in, norm_gain, norm_bias):
    row_mean = jnp.mean(rows_in, -1, keepdims=True)
    centred = rows_in - row_mean
    spread = jnp.mean(centred * centred, -1, keepdims=True)
    recip = lax.rsqrt(spread + EPS)
    normed = centred * recip
    return (normed * norm_gain + norm_bias, normed, recip)


def norm_backward(gradient, normed, recip, norm_gain):
    scaled = gradient * norm_gain
    inner_term = (
        scaled
        - jnp.mean(scaled, -1, keepdims=True)
        - normed * jnp.mean(scaled * normed, -1, keepdims=True)
    )
    return (inner_term * recip, jnp.sum(gradient * normed, 0), jnp.sum(gradient, 0))


def heads_first(flat, seq_count, block_rows, heads_local):
    return flat.reshape(seq_count, block_rows, heads_local, HEAD).transpose(0, 2, 1, 3)


def rows_first(split):
    seq_count, heads_local, block_rows, head_size = split.shape
    return split.transpose(0, 2, 1, 3).reshape(seq_count * block_rows, heads_local * head_size)


def score_block(queries, key_block, score_scale):
    return (
        jnp.einsum("shqe,shke->shqk", queries, key_block, preferred_element_type=jnp.float32)
        * score_scale
    )


def absorb(running, scores, allowed, value_block):
    row_top, denominator, weighted = running
    masked = jnp.where(allowed, scores, NEG)
    new_top = jnp.maximum(row_top, jnp.max(masked, -1))
    factor = jnp.exp(row_top - new_top)
    weights = jnp.where(allowed, jnp.exp(scores - new_top[..., None]), 0.0)
    denominator = denominator * factor + jnp.sum(weights, -1)
    weighted = weighted * factor[..., None] + jnp.einsum(
        "shqk,shke->shqe", weights, value_block.astype(jnp.float32), precision=FULL_PRECISION
    )
    return (new_top, denominator, weighted)


def block_grads(
    queries, attended_grad, row_delta, log_total, key_block, value_block, allowed, score_scale
):
    scores = score_block(queries, key_block, score_scale)
    weights = jnp.where(allowed, jnp.exp(scores - log_total[..., None]), 0.0)
    value_grad = jnp.einsum(
        "shqk,shqe->shke", weights, attended_grad.astype(jnp.float32), precision=FULL_PRECISION
    )
    inner_term = jnp.einsum(
        "shqe,shke->shqk", attended_grad, value_block, preferred_element_type=jnp.float32
    )
    score_grad = (weights * (inner_term - row_delta[..., None])).astype(jnp.bfloat16)
    query_grad = (
        jnp.einsum("shqk,shke->shqe", score_grad, key_block, preferred_element_type=jnp.float32)
        * score_scale
    )
    key_grad = (
        jnp.einsum("shqk,shqe->shke", score_grad, queries, preferred_element_type=jnp.float32)
        * score_scale
    )
    return (query_grad, key_grad, value_grad)


def per_device(
    tokens, ln_gain, ln_bias, w_qkv, qv_bias, w_out, branch_bias, w_up, up_bias, w_down, out_grad
):
    section_index = lax.axis_index("section")
    cycle_place = lax.axis_index("ctx")
    cycle_count = lax.axis_size("ctx")
    seq_count = tokens.shape[0]
    block_rows = tokens.shape[2]
    model_width = tokens.shape[3]
    head_width = w_out.shape[1]
    heads_local = head_width // HEAD
    flat_rows = seq_count * block_rows
    score_scale = HEAD ** (-0.5)
    gathered = (
        lax.all_gather(w_qkv, ("ctx", "dp"), axis=1, tiled=True),
        lax.all_gather(w_out, ("ctx", "dp"), axis=2, tiled=True),
        lax.all_gather(w_up, ("ctx", "dp"), axis=1, tiled=True),
        lax.all_gather(w_down, ("ctx", "dp"), axis=2, tiled=True),
    )
    weight_qkv = gathered[0][0]
    weight_out = gathered[1][0]
    weight_up = gathered[2][0]
    weight_down = gathered[3][0]
    norm_gain = ln_gain[0]
    norm_bias = ln_bias[0]
    query_value_bias = qv_bias[0]
    branch_terms = branch_bias[0]
    hidden_bias = up_bias[0]
    query_pos = cycle_place * block_rows + lax.broadcasted_iota(
        jnp.int32, (block_rows, block_rows), 0
    )
    key_offsets = lax.broadcasted_iota(jnp.int32, (block_rows, block_rows), 1)
    store_shape = (seq_count, heads_local, cycle_count, block_rows, HEAD)
    flat_keys = (seq_count, heads_local, cycle_count * block_rows, HEAD)

    def head_total(partial_sum):
        return lax.psum(partial_sum.astype(jnp.bfloat16), "tp").astype(jnp.float32)

    def feature_total(partial_sum):
        return lax.psum(partial_sum.astype(jnp.bfloat16), "tp").astype(jnp.float32)

    def split_heads(flat):
        return heads_first(flat, seq_count, block_rows, heads_local)

    def layer_backward(
        upstream, kept, early_keys, early_values, use_early, carried_keys, carried_values
    ):
        (
            normed_low,
            normed_one,
            recip_one,
            queries,
            key_heads,
            value_heads,
            attended,
            log_total,
            attended_low,
            normed_two,
            recip_two,
            second_low,
            hidden_pre,
            hidden_low,
            own_keys,
            own_values,
        ) = kept
        upstream_low = upstream.astype(jnp.bfloat16)
        grad_down = jnp.einsum(
            "nf,nd->fd", hidden_low, upstream_low, preferred_element_type=jnp.float32
        )
        grad_down_bias = jnp.sum(upstream, 0)
        hidden_grad = jnp.einsum(
            "nd,fd->nf", upstream_low, weight_down, preferred_element_type=jnp.float32
        )
        gelu_pull = jax.vjp(lambda inner_in: jax.nn.gelu(inner_in, approximate=True), hidden_pre)[1]
        hidden_pre_grad = gelu_pull(hidden_grad)[0].astype(jnp.bfloat16)
        grad_up = jnp.einsum(
            "nd,nf->df", second_low, hidden_pre_grad, preferred_element_type=jnp.float32
        )
        grad_up_bias = jnp.sum(hidden_pre_grad.astype(jnp.float32), 0)
        second_grad = feature_total(
            jnp.einsum("nf,df->nd", hidden_pre_grad, weight_up, preferred_element_type=jnp.float32)
        )
        mixed_part, gain_two, bias_two = norm_backward(
            second_grad, normed_two, recip_two, norm_gain[1]
        )
        mixed_grad = upstream + mixed_part
        branch_low = mixed_grad.astype(jnp.bfloat16)
        grad_out = jnp.einsum(
            "nf,nd->fd", attended_low, branch_low, preferred_element_type=jnp.float32
        )
        grad_out_bias = jnp.sum(branch_low.astype(jnp.float32), 0)
        attended_grad = split_heads(
            jnp.einsum(
                "nd,fd->nf", branch_low, weight_out, preferred_element_type=jnp.float32
            ).astype(jnp.bfloat16)
        )
        row_delta = jnp.sum(attended_grad.astype(jnp.float32) * attended, -1)
        query_grad, early_key_grad, early_value_grad = block_grads(
            queries,
            attended_grad,
            row_delta,
            log_total,
            early_keys.reshape(flat_keys),
            early_values.reshape(flat_keys),
            use_early,
            score_scale,
        )
        share_keys, share_values = (
            lax.psum_scatter(
                early_key_grad.reshape(store_shape).astype(jnp.bfloat16),
                "ctx",
                scatter_dimension=2,
                tiled=True,
            ).astype(jnp.float32),
            lax.psum_scatter(
                early_value_grad.reshape(store_shape).astype(jnp.bfloat16),
                "ctx",
                scatter_dimension=2,
                tiled=True,
            ).astype(jnp.float32),
        )
        key_block, value_block = (key_heads, value_heads)
        key_grad = jnp.zeros((seq_count, heads_local, block_rows, HEAD), jnp.float32)
        value_grad = jnp.zeros((seq_count, heads_local, block_rows, HEAD), jnp.float32)
        for cycle_step in range(cycle_count):
            source = (cycle_place - cycle_step) % cycle_count
            allowed = source * block_rows + key_offsets <= query_pos
            step_query, step_key, step_value = block_grads(
                queries,
                attended_grad,
                row_delta,
                log_total,
                key_block,
                value_block,
                allowed,
                score_scale,
            )
            query_grad = query_grad + step_query
            key_grad = key_grad + step_key
            value_grad = value_grad + step_value
            if cycle_step < cycle_count - 1:
                key_block, value_block = passed_along((key_block, value_block), "ctx", 1)
            key_grad, value_grad = (
                from_behind(key_grad.astype(jnp.bfloat16), "ctx", 1).astype(key_grad.dtype),
                from_behind(value_grad.astype(jnp.bfloat16), "ctx", 1).astype(value_grad.dtype),
            )
        key_total = key_grad + carried_keys[:, :, 0]
        value_total = value_grad + carried_values[:, :, 0]
        query_low = rows_first(query_grad).astype(jnp.bfloat16)
        key_low = rows_first(key_total).astype(jnp.bfloat16)
        value_low = rows_first(value_total).astype(jnp.bfloat16)
        stacked = jnp.stack((query_low, key_low, value_low), 1)
        grad_qkv = jnp.einsum(
            "nd,nkf->dkf", normed_low, stacked, preferred_element_type=jnp.float32
        )
        grad_qv_bias = jnp.stack(
            (jnp.sum(query_low.astype(jnp.float32), 0), jnp.sum(value_low.astype(jnp.float32), 0))
        )
        first_grad = feature_total(
            jnp.einsum("nkf,dkf->nd", stacked, weight_qkv, preferred_element_type=jnp.float32)
        )
        input_part, gain_one, bias_one = norm_backward(
            first_grad, normed_one, recip_one, norm_gain[0]
        )
        input_grad = mixed_grad + input_part
        large = (grad_qkv, grad_out, grad_up, grad_down)
        small = (
            jnp.stack((gain_one, gain_two)),
            jnp.stack((bias_one, bias_two)),
            grad_qv_bias,
            jnp.stack((grad_out_bias, grad_down_bias)),
            grad_up_bias,
        )
        return (input_grad, large, small, share_keys, share_values)

    zero_store = jnp.zeros(store_shape, jnp.bfloat16)
    early_keys, early_values = (zero_store, zero_store)
    incoming = jnp.zeros((seq_count, block_rows, model_width), jnp.bfloat16)
    kept_ticks = []
    early_ticks = []
    first_block = incoming
    sent = incoming
    for step_index in range(3):
        section_in = jnp.where(section_index == 0, tokens[:, min(step_index, 1)], incoming)
        use_early = step_index - section_index == 1
        layer_in = section_in.astype(jnp.float32).reshape(flat_rows, model_width)
        first_out, layer_normed_one, layer_recip_one = norm_forward(
            layer_in, norm_gain[0], norm_bias[0]
        )
        layer_normed_low = first_out.astype(jnp.bfloat16)
        projected = jnp.einsum(
            "nd,dkf->nkf", layer_normed_low, weight_qkv, preferred_element_type=jnp.float32
        )
        layer_queries = split_heads((projected[:, 0] + query_value_bias[0]).astype(jnp.bfloat16))
        layer_key_heads = split_heads(projected[:, 1].astype(jnp.bfloat16))
        layer_value_heads = split_heads(
            (projected[:, 2] + query_value_bias[1]).astype(jnp.bfloat16)
        )
        running = (
            jnp.full((seq_count, heads_local, block_rows), NEG, jnp.float32),
            jnp.zeros((seq_count, heads_local, block_rows), jnp.float32),
            jnp.zeros((seq_count, heads_local, block_rows, HEAD), jnp.float32),
        )
        running = absorb(
            running,
            score_block(layer_queries, early_keys.reshape(flat_keys), score_scale),
            use_early,
            early_values.reshape(flat_keys),
        )
        layer_own_keys = jnp.zeros(store_shape, jnp.bfloat16)
        layer_own_values = jnp.zeros(store_shape, jnp.bfloat16)
        layer_key_block = layer_key_heads
        layer_value_block = layer_value_heads
        for layer_cycle_step in range(cycle_count):
            layer_source = (cycle_place - layer_cycle_step) % cycle_count
            layer_allowed = layer_source * block_rows + key_offsets <= query_pos
            running = absorb(
                running,
                score_block(layer_queries, layer_key_block, score_scale),
                layer_allowed,
                layer_value_block,
            )
            layer_own_keys = lax.dynamic_update_slice_in_dim(
                layer_own_keys, layer_key_block[:, :, None], layer_source, 2
            )
            layer_own_values = lax.dynamic_update_slice_in_dim(
                layer_own_values, layer_value_block[:, :, None], layer_source, 2
            )
            if layer_cycle_step < cycle_count - 1:
                layer_key_block, layer_value_block = from_behind(
                    (layer_key_block, layer_value_block), "ctx", 1
                )
        row_top, denominator, weighted = running
        layer_attended = weighted / denominator[..., None]
        layer_log_total = row_top + jnp.log(denominator)
        layer_attended_low = rows_first(layer_attended).astype(jnp.bfloat16)
        mixed = (
            layer_in
            + head_total(
                jnp.dot(layer_attended_low, weight_out, preferred_element_type=jnp.float32)
            )
            + branch_terms[0]
        )
        second_out, layer_normed_two, layer_recip_two = norm_forward(
            mixed, norm_gain[1], norm_bias[1]
        )
        layer_second_low = second_out.astype(jnp.bfloat16)
        layer_hidden_pre = (
            jnp.dot(layer_second_low, weight_up, preferred_element_type=jnp.float32) + hidden_bias
        )
        layer_hidden_low = jax.nn.gelu(layer_hidden_pre, approximate=True).astype(jnp.bfloat16)
        result = (
            mixed
            + head_total(jnp.dot(layer_hidden_low, weight_down, preferred_element_type=jnp.float32))
            + branch_terms[1]
        )
        layer_kept = (
            layer_normed_low,
            layer_normed_one,
            layer_recip_one,
            layer_queries,
            layer_key_heads,
            layer_value_heads,
            layer_attended,
            layer_log_total,
            layer_attended_low,
            layer_normed_two,
            layer_recip_two,
            layer_second_low,
            layer_hidden_pre,
            layer_hidden_low,
            layer_own_keys,
            layer_own_values,
        )
        result, kept = (result, layer_kept)
        kept_ticks.append(kept)
        early_ticks.append((early_keys, early_values))
        early_keys, early_values = (kept[14], kept[15])
        sent = result.astype(jnp.bfloat16).reshape(seq_count, block_rows, model_width)
        if step_index < 2:
            incoming = from_behind(sent, "section", 1)
        if step_index == 1:
            first_block = incoming
    block_out = jnp.where(section_index == 0, first_block, sent)[:, None]
    carried_keys = jnp.zeros((seq_count, heads_local, 1, block_rows, HEAD), jnp.float32)
    carried_values = carried_keys
    incoming_grad = jnp.zeros((seq_count, block_rows, model_width), jnp.bfloat16)
    second_block = incoming_grad
    sent_grad = incoming_grad
    large_sum = None
    small_sum = None
    for step_index in range(3):
        own_grad = out_grad[:, max(1 - step_index, 0)]
        upstream = (
            jnp.where(section_index == 1, own_grad, incoming_grad)
            .astype(jnp.float32)
            .reshape(flat_rows, model_width)
        )
        early_keys, early_values = early_ticks[2 - step_index]
        use_early = 2 - step_index - section_index == 1
        live = jnp.where(
            (step_index + section_index >= 1) & (step_index + section_index <= 2), 1.0, 0.0
        ).astype(jnp.float32)
        input_grad, large, small, carried_keys, carried_values = layer_backward(
            upstream,
            kept_ticks[2 - step_index],
            early_keys,
            early_values,
            use_early,
            carried_keys,
            carried_values,
        )
        large = tuple((member * live for member in large))
        small = tuple((member * live for member in small))
        large_sum = large if large_sum is None else jax.tree.map(jnp.add, large_sum, large)
        small_sum = small if small_sum is None else jax.tree.map(jnp.add, small_sum, small)
        sent_grad = input_grad.astype(jnp.bfloat16).reshape(seq_count, block_rows, model_width)
        if step_index < 2:
            incoming_grad = from_behind(sent_grad, "section", -1)
        if step_index == 1:
            second_block = incoming_grad
    tokens_grad = jnp.where(section_index == 0, sent_grad, second_block)[:, None]
    shares = (
        lax.psum_scatter(
            large_sum[0][None].astype(jnp.bfloat16), ("ctx", "dp"), scatter_dimension=1, tiled=True
        ).astype(jnp.float32),
        lax.psum_scatter(
            large_sum[1][None].astype(jnp.bfloat16), ("ctx", "dp"), scatter_dimension=2, tiled=True
        ).astype(jnp.float32),
        lax.psum_scatter(
            large_sum[2][None].astype(jnp.bfloat16), ("ctx", "dp"), scatter_dimension=1, tiled=True
        ).astype(jnp.float32),
        lax.psum_scatter(
            large_sum[3][None].astype(jnp.bfloat16), ("ctx", "dp"), scatter_dimension=2, tiled=True
        ).astype(jnp.float32),
    )
    small_total = (
        lax.psum(small_sum[0].astype(jnp.bfloat16), ("ctx", "dp")).astype(jnp.float32),
        lax.psum(small_sum[1].astype(jnp.bfloat16), ("ctx", "dp")).astype(jnp.float32),
        lax.psum(small_sum[2].astype(jnp.bfloat16), ("ctx", "dp")).astype(jnp.float32),
        lax.psum(small_sum[3].astype(jnp.bfloat16), ("ctx", "dp")).astype(jnp.float32),
        lax.psum(small_sum[4].astype(jnp.bfloat16), ("ctx", "dp")).astype(jnp.float32),
    )
    return (
        block_out,
        tokens_grad,
        small_total[0][None],
        small_total[1][None],
        shares[0],
        small_total[2][None],
        shares[1],
        small_total[3][None],
        shares[2],
        small_total[4][None],
        shares[3],
    )


def solution(mesh):
    return jax.shard_map(
        per_device,
        mesh=mesh,
        in_specs=(
            P("dp", None, "ctx", None),
            P("section", None, None),
            P("section", None, None),
            P("section", ("ctx", "dp"), None, "tp"),
            P("section", None, "tp"),
            P("section", "tp", ("ctx", "dp")),
            P("section", None, None),
            P("section", ("ctx", "dp"), "tp"),
            P("section", "tp"),
            P("section", "tp", ("ctx", "dp")),
            P("dp", None, "ctx", None),
        ),
        out_specs=(
            P("dp", "section", "ctx", None),
            P("dp", "section", "ctx", None),
            P("section", None, None),
            P("section", None, None),
            P("section", ("ctx", "dp"), None, "tp"),
            P("section", None, "tp"),
            P("section", "tp", ("ctx", "dp")),
            P("section", None, None),
            P("section", ("ctx", "dp"), "tp"),
            P("section", "tp"),
            P("section", "tp", ("ctx", "dp")),
        ),
        check_vma=False,
    )
```

profile of v0, /device:TPU:0, one launch (start us, length us, event | category | flops | bytes accessed | tf_op | source)
XLA Modules:
  0.0 1464.0 jit_solution(6147979599737632688)
XLA Ops:
  13.9 46.2 %all-gather.5.cloned.1.call-done = bf16[1,1280,3,640]{3,1,2,0:T(8,128)(2,1)} async-done(((bf16[1,40,3,640]{3,1,2,0:T(8,128)(2,1)}), bf16[1,1280,3,640]{3,1,2,0:T(8,128)(2,1)}) %all-gather.5.cloned.1.call-update) | async-done | bytes 4915216 | tf_op jit(solution)/shard_map/all_gather | solution.py:110
  94.8 10.3 all-gather.7.cloned.1.call-done
  109.2 29.0 %all-reduce.19.cloned.1.call-done = bf16[128,1280]{1,0:T(8,128)(2,1)} async-done(((bf16[128,1280]{1,0:T(8,128)(2,1)}), bf16[128,1280]{1,0:T(8,128)(2,1)}) %all-reduce.19.cloned.1.call-update) | async-done | bytes 327696 | tf_op jit(solution)/shard_map/psum | solution.py:132
  140.7 50.6 %all-gather.9.cloned.1.call-done = bf16[1,1280,2560]{2,1,0:T(8,128)(2,1)} async-done(((bf16[1,40,2560]{2,1,0:T(8,128)(2,1)}), bf16[1,1280,2560]{2,1,0:T(8,128)(2,1)}) %all-gather.9.cloned.1.call-update) | async-done | bytes 6553616 | tf_op jit(solution)/shard_map/all_gather | solution.py:112
  195.5 46.6 %all-gather.11.cloned.1.call-done = bf16[1,2560,1280]{1,2,0:T(8,128)(2,1)} async-done(((bf16[1,2560,40]{1,2,0:T(8,128)(2,1)}), bf16[1,2560,1280]{1,2,0:T(8,128)(2,1)}) %all-gather.11.cloned.1.call-update) | async-done | bytes 6553616 | tf_op jit(solution)/shard_map/all_gather | solution.py:113
  248.0 29.8 %all-reduce.21.cloned.1.call-done = bf16[128,1280]{1,0:T(8,128)(2,1)} async-done(((bf16[128,1280]{1,0:T(8,128)(2,1)}), bf16[128,1280]{1,0:T(8,128)(2,1)}) %all-reduce.21.cloned.1.call-update) | async-done | bytes 327696 | tf_op jit(solution)/shard_map/psum | solution.py:132
  378.8 29.3 %all-reduce.23.cloned.1.call-done = bf16[128,1280]{1,0:T(8,128)(2,1)} async-done(((bf16[128,1280]{1,0:T(8,128)(2,1)}), bf16[128,1280]{1,0:T(8,128)(2,1)}) %all-reduce.23.cloned.1.call-update) | async-done | bytes 327696 | tf_op jit(solution)/shard_map/psum | solution.py:132
  419.5 32.0 %all-reduce.25.cloned.1.call-done = bf16[128,1280]{1,0:T(8,128)(2,1)} async-done(((bf16[128,1280]{1,0:T(8,128)(2,1)}), bf16[128,1280]{1,0:T(8,128)(2,1)}) %all-reduce.25.cloned.1.call-update) | async-done | bytes 327696 | tf_op jit(solution)/shard_map/psum | solution.py:132
  459.9 8.5 dynamic_update_slice.56
  469.5 8.5 dynamic_update_slice.60
  480.4 8.5 dynamic_update_slice.57
  488.9 8.5 dynamic_update_slice.61
  499.9 8.5 dynamic_update_slice.58
  508.4 8.6 dynamic_update_slice.62
  518.1 8.5 dynamic_update_slice.59
  529.2 8.5 dynamic_update_slice.63
  574.9 6.8 collective-permute-done.18
  602.8 21.3 %all-reduce.27.cloned.1.call-done = bf16[128,1280]{1,0:T(8,128)(2,1)} async-done(((bf16[128,1280]{1,0:T(8,128)(2,1)}), bf16[128,1280]{1,0:T(8,128)(2,1)}) %all-reduce.27.cloned.1.call-update) | async-done | bytes 327696 | tf_op jit(solution)/shard_map/psum | solution.py:132
  644.8 27.4 %all-reduce.29.cloned.1.call-done = bf16[128,1280]{1,0:T(8,128)(2,1)} async-done(((bf16[128,1280]{1,0:T(8,128)(2,1)}), bf16[128,1280]{1,0:T(8,128)(2,1)}) %all-reduce.29.cloned.1.call-update) | async-done | bytes 327696 | tf_op jit(solution)/shard_map/psum | solution.py:135
  735.0 30.6 %all-reduce.31.cloned.1.call-done = bf16[128,1280]{1,0:T(8,128)(2,1)} async-done(((bf16[128,1280]{1,0:T(8,128)(2,1)}), bf16[128,1280]{1,0:T(8,128)(2,1)}) %all-reduce.31.cloned.1.call-update) | async-done | bytes 327696 | tf_op jit(solution)/shard_map/psum | solution.py:135
  772.1 8.2 collective-permute-done.34
  922.4 16.2 %all-reduce.35.cloned.1.call-done = bf16[128,1280]{1,0:T(8,128)(2,1)} async-done(((bf16[128,1280]{1,0:T(8,128)(2,1)}), bf16[128,1280]{1,0:T(8,128)(2,1)}) %all-reduce.35.cloned.1.call-update) | async-done | bytes 327696 | tf_op jit(solution)/shard_map/psum | solution.py:135
  980.8 6.9 convolution_multiply_fusion.2
  1005.9 6.8 convolution_multiply_fusion
  1012.7 12.6 fusion.7
  1025.3 26.6 %copy.362 = bf16[1,2560,1280]{1,0,2:T(2,128)(2,1)} copy(bf16[1,2560,1280]{2,1,0:T(8,128)(2,1)} %fusion.7) | data formatting | bytes 13107200 | tf_op jit(solution)/shard_map/convert_element_type | solution.py:429
  1085.2 7.6 copy.361
  1130.8 10.4 fusion.44
  1156.2 11.3 all-reduce.41.cloned.1.call-done
  1169.0 130.4 %all-reduce.3 = (bf16[1,2,1280]{2,1,0:T(2,128)(2,1)S(1)}, bf16[1,2,1280]{2,1,0:T(2,128)(2,1)S(1)}, bf16[1,2,640]{2,1,0:T(2,128)(2,1)S(1)}, bf16[1,2,1280]{2,1,0:T(2,128)(2,1)S(1)}, bf16[1,2560]{1,0:T(2,128)(2,1)S(1)}) all-reduce(bf16[1,2,1280]{2,1,0:T(2,128)(2,1)S(1)} %fusion.551, ...), channel_id=1, replica_groups=mesh['section'=2,'ctx'=4,'dp'=8,'tp'=2] {'ctx','dp'}, use_global_device_ids=true, to_apply=%region_79.80 | all-reduce | flops 11520 | bytes 46080 | tf_op jit(solution)/shard_map/psum | solution.py:433
  1305.6 58.9 %all-reduce.39.cloned.1.call-done = (bf16[1,1280,3,640]{3,1,2,0:T(8,128)(2,1)}, bf16[1,640,1280]{1,0,2:T(2,128)(2,1)}, bf16[1,2560,1280]{1,0,2:T(2,128)(2,1)}) async-done(((bf16[1,1280,3,640]{3,1,2,0:T(8,128)(2,1)}, bf16[1,640,1280]{1,0,2:T(2,128)(2,1)}, bf16[1,2560,1280]{1,0,2:T(2,128)(2,1)}), (bf16[1,1280,3,640]{3,1,2,0:T(8,128)(2,1)}, bf16[1,640,1280]{1,0,2:T(2,128)(2,1)}, ...) | async-done | bytes 13107216
  1370.0 85.3 %reduce-scatter.15.cloned.1.call-done = bf16[1,40,2560]{2,1,0:T(8,128)(2,1)} async-done(((bf16[1,1280,2560]{2,1,0:T(8,128)(2,1)}), bf16[1,40,2560]{2,1,0:T(8,128)(2,1)}) %reduce-scatter.15.cloned.1.call-update) | async-done | bytes 204816 | tf_op jit(solution)/shard_map/reduce_scatter | solution.py:425
  (917 shorter events, 636.5 us)
Async XLA Ops:
  7.2 52.9 %all-gather.5.cloned.1.call-start = ((), (), s32[]{:S(2)}) async-start(), calls=%async_computation.5 | async-start | bytes 5068800 | tf_op jit(solution)/shard_map/all_gather | solution.py:110
  7.9 97.2 %all-gather.7.cloned.1.call-start = ((), (), s32[]{:S(2)}) async-start(), calls=%async_computation.6 | async-start | bytes 1689600 | tf_op jit(solution)/shard_map/all_gather | solution.py:111
  8.7 129.6 %all-reduce.19.cloned.1.call-start = ((), (), s32[]{:S(2)}) async-start(), calls=%async_computation.7 | async-start | bytes 655360 | tf_op jit(solution)/shard_map/psum | solution.py:132
  107.9 83.4 %all-gather.9.cloned.1.call-start = ((), (), s32[]{:S(2)}) async-start(), calls=%async_computation.8 | async-start | bytes 6758400 | tf_op jit(solution)/shard_map/all_gather | solution.py:112
  108.5 133.7 %all-gather.11.cloned.1.call-start = ((), (), s32[]{:S(2)}) async-start(), calls=%async_computation.9 | async-start | bytes 6758400 | tf_op jit(solution)/shard_map/all_gather | solution.py:113
  109.0 168.7 %all-reduce.21.cloned.1.call-start = ((), (), s32[]{:S(2)}) async-start(), calls=%async_computation.10 | async-start | bytes 655360 | tf_op jit(solution)/shard_map/psum | solution.py:132
  247.9 160.1 %all-reduce.23.cloned.1.call-start = ((), (), s32[]{:S(2)}) async-start(), calls=%async_computation.11 | async-start | bytes 655360 | tf_op jit(solution)/shard_map/psum | solution.py:132
  279.6 58.7 %collective-permute-start.6 = (bf16[1,128,1280]{2,1,0:T(8,128)(2,1)}, bf16[1,128,1280]{2,1,0:T(8,128)(2,1)}, u32[]{:S(2)}, u32[]{:S(2)}) collective-permute-start(bf16[1,128,1280]{2,1,0:T(8,128)(2,1)} %fusion.374), channel_id=1, source_target_pairs={{0,64},{64,0},{1,65},{65,1},{2,66},{66,2},{3,67},{67,3},{4,68},{68... | collective-permute-start | bytes 983048 | tf_op jit(solution)/shard_map/ppermute | solution.py:16
  378.7 72.7 %all-reduce.25.cloned.1.call-start = ((), (), s32[]{:S(2)}) async-start(), calls=%async_computation.12 | async-start | bytes 655360 | tf_op jit(solution)/shard_map/psum | solution.py:132
  419.4 204.7 %all-reduce.27.cloned.1.call-start = ((), (), s32[]{:S(2)}) async-start(), calls=%async_computation.13 | async-start | bytes 655360 | tf_op jit(solution)/shard_map/psum | solution.py:132
  453.3 86.7 %collective-permute-start.13 = (bf16[1,128,1280]{2,1,0:T(8,128)(2,1)}, bf16[1,128,1280]{2,1,0:T(8,128)(2,1)}, u32[]{:S(2)}, u32[]{:S(2)}) collective-permute-start(bf16[1,128,1280]{2,1,0:T(8,128)(2,1)} %fusion.375), channel_id=1, source_target_pairs={{0,64},{64,0},{1,65},{65,1},{2,66},{66,2},{3,67},{67,3},{4,68},{68... | collective-permute-start | bytes 983048 | tf_op jit(solution)/shard_map/ppermute | solution.py:16
  568.9 27.4 %collective-permute-start.23 = (bf16[1,10,128,64]{2,3,1,0:T(8,128)(2,1)}, bf16[1,10,128,64]{2,3,1,0:T(8,128)(2,1)}, u32[]{:S(2)}, u32[]{:S(2)}) collective-permute-start(bf16[1,10,128,64]{2,3,1,0:T(8,128)(2,1)} %collective-permute-done.21), channel_id=1, source_target_pairs={{0,16},{16,32},{32,48},{1,17},{17,33},{33,49},{2,18},{18,34},{34,5... | collective-permute-start | bytes 491528 | tf_op jit(solution)/shard_map/ppermute | solution.py:22
  591.2 81.1 %all-reduce.29.cloned.1.call-start = ((), (), s32[]{:S(2)}) async-start(), calls=%async_computation.14 | async-start | bytes 655360 | tf_op jit(solution)/shard_map/psum | solution.py:135
  591.2 51.4 %collective-permute-start.24 = (bf16[1,10,128,64]{2,3,1,0:T(8,128)(2,1)}, bf16[1,10,128,64]{2,3,1,0:T(8,128)(2,1)}, u32[]{:S(2)}, u32[]{:S(2)}) collective-permute-start(bf16[1,10,128,64]{2,3,1,0:T(8,128)(2,1)} %collective-permute-done.22), channel_id=1, source_target_pairs={{0,16},{16,32},{32,48},{1,17},{17,33},{33,49},{2,18},{18,34},{34,5... | collective-permute-start | bytes 491528 | tf_op jit(solution)/shard_map/ppermute | solution.py:22
  596.3 97.4 %collective-permute-start.25 = (bf16[1,10,128,64]{2,3,1,0:T(8,128)(2,1)}, bf16[1,10,128,64]{2,3,1,0:T(8,128)(2,1)}, u32[]{:S(2)}, u32[]{:S(2)}) collective-permute-start(bf16[1,10,128,64]{2,3,1,0:T(8,128)(2,1)} %collective-permute-done.23), channel_id=1, source_target_pairs={{0,16},{16,32},{32,48},{1,17},{17,33},{33,49},{2,18},{18,34},{34,5... | collective-permute-start | bytes 491528 | tf_op jit(solution)/shard_map/ppermute | solution.py:22
  640.2 125.4 %all-reduce.31.cloned.1.call-start = ((), (), s32[]{:S(2)}) async-start(), calls=%async_computation.15 | async-start | bytes 655360 | tf_op jit(solution)/shard_map/psum | solution.py:135
  734.5 102.2 %all-reduce.33.cloned.1.call-start = ((), (), s32[]{:S(2)}) async-start(), calls=%async_computation.16 | async-start | bytes 655360 | tf_op jit(solution)/shard_map/psum | solution.py:135
  791.2 102.6 %reduce-scatter.9.cloned.1.call-start = ((), (), s32[]{:S(2)}) async-start(), calls=%async_computation.18 | async-start | bytes 819200 | tf_op jit(solution)/shard_map/reduce_scatter | solution.py:210
  807.4 93.1 %reduce-scatter.7.cloned.1.call-start = ((), (), s32[]{:S(2)}) async-start(), calls=%async_computation.17 | async-start | bytes 819200 | tf_op jit(solution)/shard_map/reduce_scatter | solution.py:204
  812.8 96.2 %collective-permute-start.50 = (bf16[1,10,128,64]{2,3,1,0:T(8,128)(2,1)}, bf16[1,10,128,64]{2,3,1,0:T(8,128)(2,1)}, u32[]{:S(2)}, u32[]{:S(2)}) collective-permute-start(bf16[1,10,128,64]{2,3,1,0:T(8,128)(2,1)} %bitcast.975), channel_id=1, source_target_pairs={{0,16},{16,32},{32,48},{1,17},{17,33},{33,49},{2,18},{18,34},{34,5... | collective-permute-start | bytes 491528 | tf_op jit(solution)/shard_map/ppermute | solution.py:22
  814.7 96.2 %collective-permute-start.51 = (bf16[1,10,128,64]{2,3,1,0:T(8,128)(2,1)}, bf16[1,10,128,64]{2,3,1,0:T(8,128)(2,1)}, u32[]{:S(2)}, u32[]{:S(2)}) collective-permute-start(bf16[1,10,128,64]{2,3,1,0:T(8,128)(2,1)} %copy-done.118), channel_id=1, source_target_pairs={{0,16},{16,32},{32,48},{1,17},{17,33},{33,49},{2,18},{18,34},{34,5... | collective-permute-start | bytes 491528 | tf_op jit(solution)/shard_map/ppermute | solution.py:22
  819.3 38.5 %collective-permute-start.40 = (bf16[1,10,128,64]{2,3,1,0:T(8,128)(2,1)}, bf16[1,10,128,64]{2,3,1,0:T(8,128)(2,1)}, u32[]{:S(2)}, u32[]{:S(2)}) collective-permute-start(bf16[1,10,128,64]{2,3,1,0:T(8,128)(2,1)} %collective-permute-done.38), channel_id=1, source_target_pairs={{0,16},{16,32},{32,48},{1,17},{17,33},{33,49},{2,18},{18,34},{34,5... | collective-permute-start | bytes 491528 | tf_op jit(solution)/shard_map/ppermute | solution.py:22
  836.6 101.9 %all-reduce.35.cloned.1.call-start = ((), (), s32[]{:S(2)}) async-start(), calls=%async_computation.19 | async-start | bytes 655360 | tf_op jit(solution)/shard_map/psum | solution.py:135
  908.9 143.0 %all-reduce.37.cloned.1.call-start = ((), (), s32[]{:S(2)}) async-start(), calls=%async_computation.20 | async-start | bytes 655360 | tf_op jit(solution)/shard_map/psum | solution.py:135
  915.2 48.3 %collective-permute-start.54 = (bf16[1,10,128,64]{2,3,1,0:T(8,128)(2,1)}, bf16[1,10,128,64]{2,3,1,0:T(8,128)(2,1)}, u32[]{:S(2)}, u32[]{:S(2)}) collective-permute-start(bf16[1,10,128,64]{2,3,1,0:T(8,128)(2,1)} %collective-permute-done.52), channel_id=1, source_target_pairs={{0,16},{16,32},{32,48},{1,17},{17,33},{33,49},{2,18},{18,34},{34,5... | collective-permute-start | bytes 491528 | tf_op jit(solution)/shard_map/ppermute | solution.py:22
  920.3 150.2 %collective-permute-start.55 = (bf16[1,10,128,64]{2,3,1,0:T(8,128)(2,1)}, bf16[1,10,128,64]{2,3,1,0:T(8,128)(2,1)}, u32[]{:S(2)}, u32[]{:S(2)}) collective-permute-start(bf16[1,10,128,64]{2,3,1,0:T(8,128)(2,1)} %collective-permute-done.53), channel_id=1, source_target_pairs={{0,16},{16,32},{32,48},{1,17},{17,33},{33,49},{2,18},{18,34},{34,5... | collective-permute-start | bytes 491528 | tf_op jit(solution)/shard_map/ppermute | solution.py:22
  963.4 152.0 %reduce-scatter.13.cloned.1.call-start = ((), (), s32[]{:S(2)}) async-start(), calls=%async_computation.22 | async-start | bytes 819200 | tf_op jit(solution)/shard_map/reduce_scatter | solution.py:210
  974.4 145.2 %reduce-scatter.11.cloned.1.call-start = ((), (), s32[]{:S(2)}) async-start(), calls=%async_computation.21 | async-start | bytes 819200 | tf_op jit(solution)/shard_map/reduce_scatter | solution.py:204
  995.6 171.9 %all-reduce.41.cloned.1.call-start = ((), (), s32[]{:S(2)}) async-start(), calls=%async_computation.25 | async-start | bytes 1310720 | tf_op jit(solution)/shard_map/psum | solution.py:132
  1066.3 27.3 %collective-permute-start.60 = (bf16[1,10,128,64]{2,3,1,0:T(8,128)(2,1)}, bf16[1,10,128,64]{2,3,1,0:T(8,128)(2,1)}, u32[]{:S(2)}, u32[]{:S(2)}) collective-permute-start(bf16[1,10,128,64]{2,3,1,0:T(8,128)(2,1)} %fusion.264), channel_id=1, source_target_pairs={{0,16},{16,32},{32,48},{48,0},{1,17},{17,33},{33,49},{49,1},{2,18}... | collective-permute-start | bytes 491528 | tf_op jit(solution)/shard_map/ppermute | solution.py:16
  1130.7 233.8 %all-reduce.39.cloned.1.call-start = ((), (), s32[]{:S(2)}) async-start(), calls=%async_computation.24 | async-start | bytes 42598400
  1141.2 314.1 %reduce-scatter.15.cloned.1.call-start = ((), (), s32[]{:S(2)}) async-start(), calls=%async_computation.23 | async-start | bytes 6758400 | tf_op jit(solution)/shard_map/reduce_scatter | solution.py:425
  (247 other events, 4108.7 us)
Sparse Core Ops, SparseCore 0:
  10.4 49.6 all-gather.4
  62.4 42.6 all-gather.6
  108.1 30.0 all-reduce.18
  140.6 50.6 all-gather.8
  193.7 48.4 all-gather.10
  248.1 29.6 all-reduce.20
  378.9 29.1 all-reduce.22
  419.6 31.8 all-reduce.24
  591.3 32.7 all-reduce.26
  640.4 31.8 all-reduce.28
  734.7 30.9 all-reduce.30
  791.3 31.8 all-reduce.32
  825.6 23.0 reduce-scatter.8
  850.9 22.2 reduce-scatter.6
  909.1 29.4 all-reduce.34
  963.6 31.8 all-reduce.36
  997.7 23.0 reduce-scatter.12
  1023.0 21.6 reduce-scatter.10
  1130.8 36.6 all-reduce.40
  1172.2 192.1 all-reduce.38
  1368.7 86.5 reduce-scatter.14
where the time goes:
time: 1480 us; the launch traced here: 1460 us
  waiting for transfers between devices  640 us (43%)
  matrix products  270 us (18%)
  local copies, waits for them, and re-layouts  231 us (16%)
  blocking collectives  130 us (9%)
  starting transfers between devices  101 us (7%)
  other arithmetic  73 us (5%)
  between operations  18.4 us (1%)
    psum x6, waiting for transfers between devices, head_total(): return lax.psum(partial_sum.astype(jnp.bfloat16), 'tp').astype(jnp.float32)  153 us
    psum x1, blocking collectives, per_device(): lax.psum(small_sum[0].astype(jnp.bfloat16), ('ctx', 'dp'))  130 us
    ppermute x46, waiting for transfers between devices, from_behind(): lax.ppermute(shard, axis, [(i, (i + by) % length) for i in range(length)])  110 us
    reduce_scatter x1, waiting for transfers between devices, per_device(): lax.psum_scatter(large_sum[2][None].astype(jnp.bfloat16), ('ctx', 'dp'),...  85.3 us
    psum x5, waiting for transfers between devices, feature_total(): return lax.psum(partial_sum.astype(jnp.bfloat16), 'tp').astype(jnp.float32)  74.3 us
    unnamed x22, waiting for transfers between devices  61.6 us
    dynamic_update_slice x8, local copies, waits for them, and re-layouts, per_device(): lax.dynamic_update_slice_in_dim(layer_own_keys, layer_key_block[:, :, Non...  59.3 us
    dynamic_update_slice x8, local copies, waits for them, and re-layouts, per_device(): lax.dynamic_update_slice_in_dim(layer_own_values, layer_value_block[:, :,...  59.3 us
  transfers between devices with their start and end apart: 85, of which 47 were waited for; matrix products, arithmetic and copies ran while one was open for 34% of the time, Pallas kernels for 0%

commit v1 on v0

v1 whole, which is shorter than its diff:
```python
import jax
import jax.numpy as jnp
from jax import lax
from jax.experimental import pallas as pl
from jax.experimental.pallas import tpu as pltpu
from jax.sharding import PartitionSpec as P

MESH = pl.DeviceIdType.MESH
F32 = jnp.float32
BF16 = jnp.bfloat16
D = 1280
HEAD = 64
HEADS = 5
ROWS = 64
KV, QO, UP, DOWN, COLS = (0, 640, 1280, 2560, 3840)
OWN = 40
CHIP = 80
HALF = 1920
CUT = 1024
EPS = 1e-05
NEG = -1e30
MIB = 2**20


class Place:
    def __init__(self):
        self.s = lax.axis_index("section")
        self.z = lax.axis_index("ctx")
        self.dp = lax.axis_index("dp")
        self.t = lax.axis_index("tp")
        self.x = self.dp // 2
        self.c = self.dp % 2

    def core(self):
        return (self.s, self.z, self.x * 2 + 1 - self.c, self.t)

    def pair(self):
        return (self.s, self.z, self.dp, 1 - self.t)

    def other(self):
        return (1 - self.s, self.z, self.dp, self.t)

    def away(self, dz, dx):
        return (self.s, (self.z + dz + 4) % 4, (self.x + dx + 4) % 4 * 2 + self.c, self.t)

    def at(self, s, seq, t):
        return (s, self.z, self.x * 2 + seq, t)


def send(source, target, sems, device):
    copy = pltpu.make_async_remote_copy(
        src_ref=source,
        dst_ref=target,
        send_sem=sems[0],
        recv_sem=sems[1],
        device_id=device,
        device_id_type=MESH,
    )
    copy.start()
    return copy


def greet(devices):
    barrier = pltpu.get_barrier_semaphore()
    for device in devices:
        pl.semaphore_signal(barrier, inc=1, device_id=device, device_id_type=MESH)
    return barrier


def in_turn(*stages):
    live = list(stages)
    while live:
        for stage in list(live):
            if next(stage, "end") == "end":
                live.remove(stage)


def mm(a, b):
    return lax.dot_general(a, b, (((1,), (0,)), ((), ())), preferred_element_type=F32)


def mm_nt(a, b):
    return lax.dot_general(a, b, (((1,), (1,)), ((), ())), preferred_element_type=F32)


def mm_tn(a, b):
    return lax.dot_general(a, b, (((0,), (0,)), ((), ())), preferred_element_type=F32)


def gather_kernel(shard, w, peer, core_sems, send_sems, recv_sems):
    me = Place()
    devices = [me.core()] + [me.away(dz, dx) for dz, dx in ((1, 0), (-1, 0), (0, 1), (0, -1))]
    pl.semaphore_wait(greet(devices), 5)
    swap = send(shard.at[1 - me.c], peer, (core_sems.at[0], core_sems.at[1]), me.core())
    swap.wait()
    row = pl.multiple_of((me.z * 4 + me.x) * CHIP, 16)
    for start in range(0, COLS, 640):
        columns = slice(start, start + 640)
        mine = shard[me.c, :, columns]
        theirs = peer[:, columns]
        lower = jnp.where(me.c == 0, mine, theirs)
        upper = jnp.where(me.c == 0, theirs, mine)
        w[pl.ds(row, CHIP), columns] = jnp.concatenate((lower, upper), 0).astype(BF16)

    def region(half, i, j, part):
        dz, dx = (j, i) if half == 0 else (i, j)
        top = ((me.z + dz + 4) % 4 * 4 + (me.x + dx + 4) % 4) * CHIP
        left = half * HALF + (CUT if part == 1 else 0)
        width = HALF if part is None else (CUT, HALF - CUT)[part]
        return w.at[pl.ds(pl.multiple_of(top, 16), CHIP), pl.ds(left, width)]

    def step(half, i, j, part, first, by, group, kind):
        along = (0, by) if (half == 0) == first else (by, 0)
        ref = region(half, i, j, part)
        sems = (send_sems.at[half, group, kind], recv_sems.at[half, group, kind])
        return send(ref, ref, sems, me.away(*along))

    flying = {}

    def go(half, i, j, part, first, by, group, kind):
        flying[half, group, kind] = step(half, i, j, part, first, by, group, kind)

    def across(half, group, i):
        go(half, i, 0, None, False, 1, group, 0)
        go(half, i, 0, None, False, -1, group, 1)

    def landed(half, group, kind):
        flying[half, group, kind].wait_recv()

    for half in (0, 1):
        go(half, 0, 0, None, True, 1, 0, 0)
        go(half, 0, 0, None, True, -1, 0, 1)
    for half in (0, 1):
        across(half, 1, 0)
    for half in (0, 1):
        landed(half, 0, 0)
        go(half, -1, 0, 0, True, 1, 0, 2)
        across(half, 2, -1)
        landed(half, 0, 1)
        go(half, 1, 0, 1, True, -1, 0, 3)
        across(half, 3, 1)
    for half in (0, 1):
        landed(half, 1, 0)
        go(half, 0, -1, 0, False, 1, 1, 2)
        landed(half, 1, 1)
        go(half, 0, 1, 1, False, -1, 1, 3)
    for half in (0, 1):
        landed(half, 0, 2)
        landed(half, 0, 3)
        across(half, 4, 2)
    for group, i in ((2, -1), (3, 1), (4, 2)):
        for half in (0, 1):
            landed(half, group, 0)
            go(half, i, -1, 0, False, 1, group, 2)
            landed(half, group, 1)
            go(half, i, 1, 1, False, -1, group, 3)
    for group in (1, 2, 3, 4):
        for half in (0, 1):
            landed(half, group, 2)
            landed(half, group, 3)
    for copy in flying.values():
        copy.wait_send()


def scatter_kernel(
    grads,
    home_sum,
    quarter_sum,
    out_rows,
    grad_rows,
    shares,
    home_total,
    quarter_total,
    out_block,
    grad_block,
    landing,
    passing,
    first_sums,
    reduced,
    from_core,
    small,
    small_in,
    send_sems,
    recv_sems,
    core_sems,
    small_send,
    small_recv,
    rows_send,
    rows_recv,
):
    me = Place()
    devices = [me.core(), me.pair()]
    devices += [me.away(dz, dx) for dz, dx in ((1, 0), (2, 0), (3, 0), (0, 1), (0, 2), (0, 3))]
    barrier = greet(devices)
    kinds = ((1, out_rows, out_block), (0, grad_rows, grad_block))
    for origin, _, _ in kinds:
        for seq in (0, 1):
            itself = (me.s == origin) & (me.c == seq) & (me.t == me.s)

            @pl.when(jnp.logical_not(itself))
            def _():
                pl.semaphore_signal(
                    barrier, inc=1, device_id=me.at(origin, seq, me.s), device_id_type=MESH
                )

    pl.semaphore_wait(barrier, 8 + 4 - (me.t == me.s).astype(jnp.int32))

    def rows_copies(kind, act):
        origin, source, target = kinds[kind]

        @pl.when(me.s == origin)
        def _():
            for seq in (0, 1):
                for t in (0, 1):
                    itself = (me.t == me.s) & (me.c == seq) & (me.t == t)
                    place = target.at[pl.ds(pl.multiple_of(me.c * ROWS, ROWS), ROWS)]

                    @pl.when(jnp.logical_not(itself))
                    def _():
                        copy = pltpu.make_async_remote_copy(
                            src_ref=source.at[seq],
                            dst_ref=place,
                            send_sem=rows_send.at[kind, seq, t],
                            recv_sem=rows_recv.at[kind, me.c],
                            device_id=me.at(me.t, seq, t),
                            device_id_type=MESH,
                        )
                        if act == "start":
                            copy.start()
                        else:
                            copy.wait_send()

                    if act == "start":

                        @pl.when(itself)
                        def _():
                            place[...] = source[seq]

    def rows_arrive(kind):
        origin, source, target = kinds[kind]
        for seq in (0, 1):
            itself = (me.s == origin) & (me.c == seq) & (me.t == me.s)

            @pl.when(jnp.logical_not(itself))
            def _():
                pltpu.make_async_remote_copy(
                    src_ref=source.at[0],
                    dst_ref=target.at[pl.ds(seq * ROWS, ROWS)],
                    send_sem=rows_send.at[kind, 0, 0],
                    recv_sem=rows_recv.at[kind, seq],
                    device_id=me.core(),
                    device_id_type=MESH,
                ).wait_recv()

    parts = ((0, CUT), (CUT, HALF - CUT))
    flying = {}

    def go(half, group, kind, source, slot, part, by):
        first = group != 4
        along = (by, 0) if (half == 0) == first else (0, by)
        target = landing.at[half, group, slot, :, pl.ds(*parts[part])]
        sems = (send_sems.at[half, group, kind], recv_sems.at[half, group, kind])
        flying[half, group, kind] = send(source, target, sems, me.away(*along))

    def piece(half, group, j, part):
        left, width = parts[part]
        if group == 4:
            return first_sums.at[half, j % 4, :, pl.ds(left, width)]
        dz, dx = (j, group) if half == 0 else (group, j)
        top = ((me.z + dz + 4) % 4 * 4 + (me.x + dx + 4) % 4) * CHIP
        return grads.at[pl.ds(pl.multiple_of(top, 16), CHIP), pl.ds(half * HALF + left, width)]

    def begin(half, group):
        go(half, group, 0, piece(half, group, 2, 0), 0, 0, 1)
        go(half, group, 1, piece(half, group, 2, 1), 0, 1, -1)
        go(half, group, 2, piece(half, group, 1, 1), 1, 1, 1)
        go(half, group, 3, piece(half, group, -1, 0), 2, 0, -1)

    def pass_on(half, group):
        for kind, part, j, by, slot in ((0, 0, 1, 1, 1), (1, 1, -1, -1, 2)):
            flying[half, group, kind].wait_recv()
            columns = slice(parts[part][0], sum(parts[part]))
            own = piece(half, group, j, part)[...].astype(F32)
            arrived = landing[half, group, 0, :, columns].astype(F32)
            passing[half, group, :, columns] = (own + arrived).astype(BF16)
            source = passing.at[half, group, :, pl.ds(*parts[part])]
            go(half, group, 4 + kind, source, slot, part, by)

    def finish(half, group):
        for kind in (2, 3, 4, 5):
            flying[half, group, kind].wait_recv()
        for part in (0, 1):
            columns = slice(parts[part][0], sum(parts[part]))
            total = (
                piece(half, group, 0, part)[...].astype(F32)
                + landing[half, group, 1, :, columns].astype(F32)
                + landing[half, group, 2, :, columns].astype(F32)
            )
            if group == 4:
                left = half * HALF + parts[part][0]
                reduced[:, left : left + parts[part][1]] = total
            else:
                first_sums[half, group, :, columns] = total.astype(BF16)

    rows_copies(0, "start")
    rows_copies(1, "start")
    for group in (2, 1, 3):
        for half in (0, 1):
            begin(half, group)

    small[0, 0:8, :] = home_sum[...]
    small[0, 8:16, :] = quarter_sum[...]
    small_flying = []

    def small_step(step, rows, devices):
        sent = []
        for index, device in enumerate(devices):
            sems = (small_send.at[step, index], small_recv.at[step, index])
            sent.append(
                send(small.at[step, pl.ds(0, rows)], small_in.at[step, index, pl.ds(0, rows)], sems, device)
            )
        small_flying.extend(sent)
        yield
        for copy in sent:
            copy.wait_recv()
        total = small[step, 0:rows, :]
        for index in range(len(devices)):
            total = total + small_in[step, index, 0:rows, :]
        small[step + 1, 0:rows, :] = total
        if rows == 8:
            small[step + 1, 8:16, :] = small[step, 8:16, :]

    def small_steps():
        yield from small_step(0, 8, [me.core()])
        yield from small_step(1, 8, [me.pair()])
        yield from small_step(2, 16, [me.away(0, dx) for dx in (1, 2, 3)])
        yield from small_step(3, 16, [me.away(dz, 0) for dz in (1, 2, 3)])

    smalls = small_steps()
    next(smalls)
    for group in (0,):
        for half in (0, 1):
            begin(half, group)
    for group in (2, 1, 3):
        for half in (0, 1):
            pass_on(half, group)
        next(smalls, None)
    for half in (0, 1):
        pass_on(half, 0)
    for group in (2, 1, 3):
        for half in (0, 1):
            finish(half, group)
    for half in (0, 1):
        begin(half, 4)
    for half in (0, 1):
        finish(half, 0)
    for half in (0, 1):
        pass_on(half, 4)
    next(smalls, None)
    home_total[...] = small[4, 0:8, :]
    quarter_total[me.c] = small[4, 8:16, :]
    sems = (core_sems.at[2], core_sems.at[3])
    vector_swap = send(small.at[4, pl.ds(8, 8)], quarter_total.at[me.c], sems, me.core())
    for half in (0, 1):
        finish(half, 4)
    theirs = pl.ds(pl.multiple_of((1 - me.c) * OWN, 8), OWN)
    sems = (core_sems.at[0], core_sems.at[1])
    swap = send(reduced.at[theirs], shares.at[me.c], sems, me.core())
    shares[me.c] = reduced[pl.ds(pl.multiple_of(me.c * OWN, 8), OWN), :]
    rows_arrive(0)
    rows_arrive(1)
    swap.wait()
    vector_swap.wait()
    for copy in flying.values():
        copy.wait_send()
    for copy in small_flying:
        copy.wait_send()
    rows_copies(0, "wait")
    rows_copies(1, "wait")


def layers_kernel(
    tokens,
    out_grad,
    w,
    ln_gain,
    ln_bias,
    kv_bias,
    qo_bias,
    branch_bias,
    up_bias,
    grads,
    out_rows,
    grad_rows,
    home_sum,
    quarter_sum,
    x_in,
    g_in,
    a_all,
    c_all,
    g_all,
    ga_all,
    q_pad,
    kv_all,
    probs_one,
    probs_two,
    o_all,
    u_all,
    hidden,
    du_all,
    go_pad,
    dqkv,
    dkv_part,
    dkv_in,
    dkv_pass,
    part,
    core_in,
    pair_out,
    pair_in,
    normed,
    recips,
    turned,
    sems_s,
    sems_r,
    hop_sems,
):
    me = Place()
    devices = [me.core(), me.pair(), me.away(1, 0), me.away(-1, 0), me.other()]
    pl.semaphore_wait(greet(devices), 5)
    counter = {0: 0, 1: 0}

    def new_sems(seq):
        index = counter[seq]
        counter[seq] = index + 1
        return (sems_s.at[seq, index], sems_r.at[seq, index])

    flying = []

    def fly(source, target, seq, device):
        copy = send(source, target, new_sems(seq), device)
        flying.append(copy)
        return copy

    lanes = lax.broadcasted_iota(jnp.int32, (256, 640), 1) % 128
    low_lanes = lanes < HEAD

    def first_rows(section, whole, rows_in):
        @pl.when(me.s == section)
        def _():
            mine = pl.ds(pl.multiple_of(me.c * ROWS, ROWS), ROWS)
            theirs = pl.ds(pl.multiple_of((1 - me.c) * ROWS, ROWS), ROWS)
            sems = (hop_sems.at[0, section, me.c], hop_sems.at[1, section, me.c])
            copy = send(whole.at[me.t, theirs], rows_in.at[me.c], sems, me.core())
            rows_in[me.c] = whole[me.t, mine, :]
            copy.wait_send()

    def rows_ready(section, whole, rows_in, seq):
        @pl.when(jnp.logical_not((me.s == section) & (me.c == seq)))
        def _():
            pltpu.make_async_remote_copy(
                src_ref=rows_in.at[seq],
                dst_ref=rows_in.at[seq],
                send_sem=hop_sems.at[0, section, seq],
                recv_sem=hop_sems.at[1, section, seq],
                device_id=me.core(),
                device_id_type=MESH,
            ).wait_recv()

    def hop(section, rows_out, rows_in, seq):
        @pl.when(me.s == section)
        def _():
            sems = (hop_sems.at[2, section, seq], hop_sems.at[1, section, seq])
            send(rows_out.at[seq], rows_in.at[seq], sems, me.other()).wait_send()

    def spread(rows, seq):
        own = rows.at[seq, me.t, me.c]
        pair = fly(own, own, seq, me.pair())
        core = fly(own, own, seq, me.core())
        yield
        pair.wait_recv()
        arrived = rows.at[seq, 1 - me.t, me.c]
        further = fly(arrived, arrived, seq, me.core())
        yield
        core.wait_recv()
        further.wait_recv()

    parts_flying = {0: [], 1: []}

    def before_part(seq):
        for copy in parts_flying[seq]:
            copy.wait_send()
        parts_flying[seq] = []

    def collect(which, seq):
        arriving = core_in.at[seq, which]
        core = send(part.at[seq, :, 1 - me.c], arriving, new_sems(seq), me.core())
        parts_flying[seq].append(core)
        yield
        core.wait_recv()
        theirs = part[seq, 1 - me.t, me.c].astype(F32) + core_in[seq, which, 1 - me.t].astype(F32)
        pair_out[seq, which] = theirs.astype(BF16)
        pair = fly(pair_out.at[seq, which], pair_in.at[seq, which], seq, me.pair())
        mine = part[seq, me.t, me.c].astype(F32) + core_in[seq, which, me.t].astype(F32)
        yield
        pair.wait_recv()
        return mine + pair_in[seq, which].astype(F32)

    def norm(rows, which, seq, target):
        centred = rows - jnp.mean(rows, -1, keepdims=True)
        recip = lax.rsqrt(jnp.mean(centred * centred, -1, keepdims=True) + EPS)
        units = centred * recip
        normed[seq, which] = units
        recips[seq, which] = recip
        out = units * ln_gain[which : which + 1, :] + ln_bias[which : which + 1, :]
        target[seq, me.t, me.c] = out.astype(BF16)

    def norm_back(grad, which, seq):
        units = normed[seq, which]
        scaled = grad * ln_gain[which : which + 1, :]
        inner = (
            scaled
            - jnp.mean(scaled, -1, keepdims=True)
            - units * jnp.mean(scaled * units, -1, keepdims=True)
        )
        home_sum[which : which + 1, :] += jnp.sum(grad * units, 0, keepdims=True)
        home_sum[2 + which : 3 + which, :] += jnp.sum(grad, 0, keepdims=True)
        return inner * recips[seq, which]

    def tiled(count, body):
        def one(n, carry):
            body(pl.multiple_of(n * 256, 256))
            return carry

        lax.fori_loop(0, count, one, 0)

    def back_through(rows, left, width, seq):
        def tile(n):
            out = mm_nt(rows, w[pl.ds(n, 256), left : left + width])
            part[seq, :, :, :, pl.ds(n, 256)] = out.reshape(2, 2, ROWS, 256).astype(BF16)

        tiled(5, tile)

    def causal(width):
        query = me.z * 128 + lax.broadcasted_iota(jnp.int32, (128, width), 0)
        key = lax.broadcasted_iota(jnp.int32, (128, width), 1) - (width - 512)
        return key <= query

    def forward(seq):
        rows_ready(0, tokens, x_in, seq)
        rows = x_in[seq].astype(F32)
        norm(rows, 0, seq, a_all)
        yield from spread(a_all, seq)
        a = a_all[seq].reshape(256, D)
        pairs = (mm(a, w[:, KV:QO]) + kv_bias[me.c]).astype(BF16)
        for head in range(HEADS):
            kv_all[seq, head, :, me.z] = pairs[:, head * 128 : head * 128 + 128].reshape(2, 128, 128)
        own = kv_all.at[seq, :, :, me.z]
        up = fly(own, own, seq, me.away(1, 0))
        down = fly(own, own, seq, me.away(-1, 0))
        queries = jnp.where(low_lanes, mm(a, w[:, QO:UP]) + qo_bias[me.c], 0.0)
        queries = (queries.astype(BF16).astype(F32) * HEAD**-0.5).astype(BF16)
        for head in range(HEADS):
            q_pad[seq, head] = queries[:, head * 128 : head * 128 + 128]
        yield
        up.wait_recv()
        arrived = kv_all.at[seq, :, 0, (me.z + 3) % 4]
        up = fly(arrived, arrived, seq, me.away(1, 0))
        down.wait_recv()
        arrived = kv_all.at[seq, :, 1, (me.z + 1) % 4]
        down = fly(arrived, arrived, seq, me.away(-1, 0))
        yield
        up.wait_recv()
        down.wait_recv()

        def one_head(head, carry):
            pairs = kv_all[seq, head].reshape(1024, 128)
            columns = pl.ds(pl.multiple_of(head * 128, 128), 128)
            high = lax.broadcasted_iota(jnp.int32, (128, 128), 1) >= HEAD
            for block, probs, width in ((0, probs_one, 512), (1, probs_two, 1024)):
                top = block * 128
                scores = mm_nt(q_pad[seq, head, top : top + 128, :], pairs[:width])
                scores = jnp.where(causal(width), scores, NEG)
                weights = jnp.exp(scores - jnp.max(scores, -1, keepdims=True))
                weights = weights / jnp.sum(weights, -1, keepdims=True)
                weights = weights.astype(BF16)
                probs[seq, head] = weights
                out = jnp.where(high, mm(weights, pairs[:width]), 0.0)
                o_all[seq, top : top + 128, columns] = out.astype(BF16)
            return carry

        lax.fori_loop(0, HEADS, one_head, 0)
        back_through(o_all[seq], QO, 640, seq)
        total = yield from collect(0, seq)
        rows = rows + total + branch_bias[0:1, :]
        norm(rows, 1, seq, c_all)
        yield from spread(c_all, seq)

        def up_tile(n):
            columns = pl.ds(n, 256)
            pre = mm(c_all[seq].reshape(256, D), w[:, pl.ds(UP + n, 256)]) + up_bias[me.c, :, columns]
            u_all[seq, :, columns] = pre
            hidden[seq, :, columns] = jax.nn.gelu(pre, approximate=True).astype(BF16)

        tiled(5, up_tile)
        before_part(seq)
        back_through(hidden[seq], DOWN, 1280, seq)
        total = yield from collect(1, seq)
        rows = rows + total + branch_bias[1:2, :]
        out_rows[seq] = rows.astype(BF16)
        hop(0, out_rows, x_in, seq)

    def backward(seq):
        rows_ready(1, out_grad, g_in, seq)
        rows = g_in[seq]
        g_all[seq, me.t, me.c] = rows
        rows = rows.astype(F32)
        home_sum[5:6, :] += jnp.sum(rows, 0, keepdims=True)
        yield from spread(g_all, seq)

        def down_tile(n):
            columns = pl.ds(n, 256)
            grad = mm(g_all[seq].reshape(256, D), w[:, pl.ds(DOWN + n, 256)])
            pre = u_all[seq, :, columns]
            scale = 0.7978845608028654
            curve = jnp.tanh(scale * (pre + 0.044715 * (pre * pre * pre)))
            slope = 0.5 * (1.0 + curve) + 0.5 * pre * (1.0 - curve * curve) * (
                scale * (1.0 + 3 * 0.044715 * (pre * pre))
            )
            grad = (grad * slope).astype(BF16)
            du_all[seq, :, columns] = grad
            quarter_sum[1:2, columns] += jnp.sum(grad.astype(F32), 0, keepdims=True)

        tiled(5, down_tile)
        before_part(seq)
        back_through(du_all[seq], UP, 1280, seq)
        total = yield from collect(2, seq)
        rows = rows + norm_back(total, 1, seq)
        low = rows.astype(BF16)
        ga_all[seq, me.t, me.c] = low
        home_sum[4:5, :] += jnp.sum(low.astype(F32), 0, keepdims=True)
        yield from spread(ga_all, seq)
        grad = mm(ga_all[seq].reshape(256, D), w[:, QO:UP])
        go_pad[seq] = jnp.where(low_lanes, 0.0, grad).astype(BF16)

        def one_head(head, carry):
            pairs = kv_all[seq, head].reshape(1024, 128)
            columns = pl.ds(pl.multiple_of(head * 128, 128), 128)
            low_half = lax.broadcasted_iota(jnp.int32, (128, 128), 1) < HEAD
            out_grads = go_pad[seq, :, columns]
            queries = q_pad[seq, head]
            score_grads = []
            weights = []
            for block, probs, width in ((0, probs_one, 512), (1, probs_two, 1024)):
                top = block * 128
                low = probs[seq, head]
                pulled = low.astype(F32) * mm_nt(out_grads[top : top + 128], pairs[:width])
                delta = jnp.sum(pulled, -1, keepdims=True)
                grad = (pulled - low.astype(F32) * delta).astype(BF16)
                query_grad = mm(grad, pairs[:width]) * HEAD**-0.5
                place = pl.ds(pl.multiple_of(QO + head * 128, 128), 128)
                dqkv[seq, top : top + 128, place] = jnp.where(low_half, query_grad, 0.0).astype(BF16)
                score_grads.append(grad)
                weights.append(low)
            early = mm_tn(jnp.concatenate((score_grads[0], score_grads[1][:, :512]), 0), queries)
            early += mm_tn(jnp.concatenate((weights[0], weights[1][:, :512]), 0), out_grads)
            late = mm_tn(score_grads[1][:, 512:], queries[128:])
            late += mm_tn(weights[1][:, 512:], out_grads[128:])
            dkv_part[seq, head, 0] = early.reshape(4, 128, 128).astype(BF16)
            dkv_part[seq, head, 1] = late.reshape(4, 128, 128).astype(BF16)
            return carry

        lax.fori_loop(0, HEADS, one_head, 0)
        far, right, left = ((me.z + 2) % 4, (me.z + 1) % 4, (me.z + 3) % 4)
        far_up = fly(dkv_part.at[seq, :, 0, far], dkv_in.at[seq, 0, :, 0], seq, me.away(1, 0))
        far_down = fly(dkv_part.at[seq, :, 1, far], dkv_in.at[seq, 0, :, 1], seq, me.away(-1, 0))
        up_own = fly(dkv_part.at[seq, :, 1, right], dkv_in.at[seq, 1, :, 1], seq, me.away(1, 0))
        down_own = fly(dkv_part.at[seq, :, 0, left], dkv_in.at[seq, 2, :, 0], seq, me.away(-1, 0))
        yield
        far_up.wait_recv()
        total = dkv_part[seq, :, 0, right].astype(F32) + dkv_in[seq, 0, :, 0].astype(F32)
        dkv_pass[seq, :, 0] = total.astype(BF16)
        up_sum = fly(dkv_pass.at[seq, :, 0], dkv_in.at[seq, 1, :, 0], seq, me.away(1, 0))
        far_down.wait_recv()
        total = dkv_part[seq, :, 1, left].astype(F32) + dkv_in[seq, 0, :, 1].astype(F32)
        dkv_pass[seq, :, 1] = total.astype(BF16)
        down_sum = fly(dkv_pass.at[seq, :, 1], dkv_in.at[seq, 2, :, 1], seq, me.away(-1, 0))
        yield
        for copy in (up_own, down_own, up_sum, down_sum):
            copy.wait_recv()
        for head in range(HEADS):
            total = (
                dkv_part[seq, head, :, me.z].astype(F32)
                + dkv_in[seq, 1, head].astype(F32)
                + dkv_in[seq, 2, head].astype(F32)
            )
            dqkv[seq, :, head * 128 : head * 128 + 128] = total.reshape(256, 128).astype(BF16)
        before_part(seq)
        back_through(dqkv[seq], KV, 1280, seq)
        yield from collect_last(seq, rows)

    def collect_last(seq, rows):
        total = yield from collect(3, seq)
        rows = rows + norm_back(total, 0, seq)
        grad_rows[seq] = rows.astype(BF16)
        hop(1, grad_rows, g_in, seq)

    home_sum[...] = jnp.zeros_like(home_sum)
    quarter_sum[...] = jnp.zeros_like(quarter_sum)
    first_rows(0, tokens, x_in)
    first_rows(1, out_grad, g_in)
    in_turn(forward(0), forward(1))
    in_turn(backward(0), backward(1))

    def grad_tiles(rows, columns, other, left, count, more):
        turned[...] = rows[...].reshape(512, D).T

        def tile(n):
            out = mm(turned[...], other[:, :, pl.ds(columns + n, 256)].reshape(512, 256))
            place = pl.ds(left + n, 256)
            if more:
                out = out + grads[:, place].astype(F32)
            grads[:, place] = out.astype(BF16)

        tiled(count, tile)

    grad_tiles(g_all, 0, hidden, DOWN, 5, False)
    grad_tiles(c_all, 0, du_all, UP, 5, False)
    grad_tiles(a_all, 0, dqkv, KV, 5, False)
    turned[...] = ga_all[...].reshape(512, D).T
    for start in (0, 256, 512):
        width = min(256, 640 - start)
        columns = slice(QO + start, QO + start + width)
        out = mm(turned[...], o_all[:, :, start : start + width].reshape(512, width))
        grads[:, columns] = (out + grads[:, columns].astype(F32)).astype(BF16)
    column_sum = jnp.sum(dqkv[...].astype(F32), axis=(0, 1))
    quarter_sum[0:1, :] += column_sum.reshape(1, D)
    for copy in flying:
        copy.wait_send()
    before_part(0)
    before_part(1)


def vmem(shape, kind):
    return pltpu.VMEM(shape, kind)


def call(kernel, name, operands, outs, scratch, collective_id, flops):
    whole = pl.BlockSpec(memory_space=pltpu.VMEM)
    moved = sum(a.size * a.dtype.itemsize for a in operands)
    return pl.pallas_call(
        kernel,
        name=name,
        out_shape=[jax.ShapeDtypeStruct(shape, kind) for shape, kind in outs],
        in_specs=[whole] * len(operands),
        out_specs=[whole] * len(outs),
        scratch_shapes=scratch,
        cost_estimate=pl.CostEstimate(flops=flops, bytes_accessed=moved, transcendentals=0),
        compiler_params=pltpu.CompilerParams(
            collective_id=collective_id, has_side_effects=True, vmem_limit_bytes=62 * MIB
        ),
    )(*operands)


def per_device(
    tokens, ln_gain, ln_bias, w_qkv, qv_bias, w_out, branch_bias, w_up, up_bias, w_down, out_grad
):
    dma = pltpu.SemaphoreType.DMA
    halves = w_qkv[0].reshape(OWN, 3, 2 * HEADS, HEAD)
    out_turned = w_out[0].T.reshape(OWN, 2 * HEADS, HEAD)
    shard = jnp.concatenate(
        (
            jnp.concatenate((halves[:, 1], halves[:, 2]), -1).reshape(OWN, 2, 640),
            jnp.concatenate((halves[:, 0], out_turned), -1).reshape(OWN, 2, 640),
            w_up[0].reshape(OWN, 2, D),
            w_down[0].T.reshape(OWN, 2, D),
        ),
        -1,
    )
    shard = shard.transpose(1, 0, 2).astype(F32)
    biases = qv_bias[0].reshape(2, 2, HEADS, HEAD)
    none = jnp.zeros((2, HEADS, HEAD), F32)
    kv_bias = jnp.concatenate((none, biases[1]), -1).reshape(2, 1, 640)
    qo_bias = jnp.concatenate((biases[0], none), -1).reshape(2, 1, 640)

    (w,) = call(
        gather_kernel,
        "gather_weights",
        [shard],
        [((D, COLS), BF16)],
        [vmem((OWN, COLS), F32), dma((2,)), dma((2, 5, 4)), dma((2, 5, 4))],
        0,
        0,
    )
    grads, out_rows, grad_rows, home_sum, quarter_sum = call(
        layers_kernel,
        "layers",
        [
            tokens[0],
            out_grad[0],
            w,
            ln_gain[0],
            ln_bias[0],
            kv_bias,
            qo_bias,
            branch_bias[0],
            up_bias[0].reshape(2, 1, D),
        ],
        [
            ((D, COLS), BF16),
            ((2, ROWS, D), BF16),
            ((2, ROWS, D), BF16),
            ((8, D), F32),
            ((8, D), F32),
        ],
        [
            vmem((2, ROWS, D), BF16),
            vmem((2, ROWS, D), BF16),
            vmem((2, 2, 2, ROWS, D), BF16),
            vmem((2, 2, 2, ROWS, D), BF16),
            vmem((2, 2, 2, ROWS, D), BF16),
            vmem((2, 2, 2, ROWS, D), BF16),
            vmem((2, HEADS, 256, 128), BF16),
            vmem((2, HEADS, 2, 4, 128, 128), BF16),
            vmem((2, HEADS, 128, 512), BF16),
            vmem((2, HEADS, 128, 1024), BF16),
            vmem((2, 256, 640), BF16),
            vmem((2, 256, D), F32),
            vmem((2, 256, D), BF16),
            vmem((2, 256, D), BF16),
            vmem((2, 256, 640), BF16),
            vmem((2, 256, D), BF16),
            vmem((2, HEADS, 2, 4, 128, 128), BF16),
            vmem((2, 3, HEADS, 2, 128, 128), BF16),
            vmem((2, HEADS, 2, 128, 128), BF16),
            vmem((2, 2, 2, ROWS, D), BF16),
            vmem((2, 4, 2, ROWS, D), BF16),
            vmem((2, 4, ROWS, D), BF16),
            vmem((2, 4, ROWS, D), BF16),
            vmem((2, 2, ROWS, D), F32),
            vmem((2, 2, ROWS, 1), F32),
            vmem((D, 512), BF16),
            dma((2, 32)),
            dma((2, 32)),
            dma((3, 2, 2)),
        ],
        1,
        2 * 512 * D * COLS * 3,
    )
    shares, home_total, quarter_total, out_block, grad_block = call(
        scatter_kernel,
        "scatter_gradients",
        [grads, home_sum, quarter_sum, out_rows, grad_rows],
        [
            ((2, OWN, COLS), F32),
            ((8, D), F32),
            ((2, 8, D), F32),
            ((2 * ROWS, D), BF16),
            ((2 * ROWS, D), BF16),
        ],
        [
            vmem((2, 5, 3, CHIP, HALF), BF16),
            vmem((2, 5, CHIP, HALF), BF16),
            vmem((2, 4, CHIP, HALF), BF16),
            vmem((CHIP, COLS), F32),
            vmem((8, D), F32),
            vmem((5, 16, D), F32),
            vmem((4, 3, 16, D), F32),
            dma((2, 5, 6)),
            dma((2, 5, 6)),
            dma((4,)),
            dma((4, 3)),
            dma((4, 3)),
            dma((2, 2, 2)),
            dma((2, 2)),
        ],
        2,
        0,
    )
    shares = shares.transpose(1, 0, 2)
    pairs = shares[:, :, KV:QO].reshape(OWN, 2 * HEADS, 2, HEAD)
    others = shares[:, :, QO:UP].reshape(OWN, 2 * HEADS, 2, HEAD)
    qkv_grad = jnp.stack((others[:, :, 0], pairs[:, :, 0], pairs[:, :, 1]), 1)
    sums = quarter_total[:, 0].reshape(2, 2, HEADS, 2, HEAD)
    qv_grad = jnp.stack((sums[:, 1, :, 0].reshape(640), sums[:, 0, :, 1].reshape(640)))
    return (
        out_block[None, None],
        grad_block[None, None],
        home_total[None, 0:2],
        home_total[None, 2:4],
        qkv_grad.reshape(1, OWN, 3, 640),
        qv_grad[None],
        others[:, :, 1].reshape(OWN, 640).T[None],
        home_total[None, 4:6],
        shares[:, :, UP:DOWN].reshape(1, OWN, 2 * D),
        quarter_total[:, 1].reshape(1, 2 * D),
        shares[:, :, DOWN:].reshape(OWN, 2 * D).T[None],
    )


def solution(mesh):
    weights = P("section", ("ctx", "dp"), None, "tp")
    up = P("section", ("ctx", "dp"), "tp")
    down = P("section", "tp", ("ctx", "dp"))
    vector = P("section", None, None)
    return jax.shard_map(
        per_device,
        mesh=mesh,
        in_specs=(
            P("dp", None, "ctx", None),
            vector,
            vector,
            weights,
            P("section", None, "tp"),
            down,
            vector,
            up,
            P("section", "tp"),
            down,
            P("dp", None, "ctx", None),
        ),
        out_specs=(
            P("dp", "section", "ctx", None),
            P("dp", "section", "ctx", None),
            vector,
            vector,
            weights,
            P("section", None, "tp"),
            down,
            vector,
            up,
            P("section", "tp"),
            down,
        ),
        check_vma=False,
    )
```

time: 1480 us -> 477 us (0.32)
  waiting for transfers between devices: 640 us -> 0 us
  Pallas kernels: 0 us -> 454 us
  matrix products: 270 us -> 0 us
  local copies, waits for them, and re-layouts: 231 us -> 18.2 us
  blocking collectives: 130 us -> 0 us
  starting transfers between devices: 101 us -> 0 us
  other arithmetic: 73 us -> 2.67 us
  between operations: 18.4 us -> 0.85 us
    pallas_call x0 -> x3, Pallas kernels: none -> 454 us  [call(): pl.pallas_call(kernel, name=name, out_shape=[jax.ShapeDtypeStruct(shape,...]
    dot_general x132 -> x0, matrix products: 270 us -> none  [the longest x14 27.8 us: block_grads(): jnp.einsum('shqk,shqe->shke', weights, attended_grad.astype(jnp.float32),...]
    psum x11 -> x0, waiting for transfers between devices: 227 us -> none  [the longest x6 153 us: head_total(): return lax.psum(partial_sum.astype(jnp.bfloat16), 'tp').astype(jnp.float32)]
    all_gather x4 -> x0, waiting for transfers between devices: 154 us -> none  [the longest x1 50.6 us: per_device(): lax.all_gather(w_up, ('ctx', 'dp'), axis=1, tiled=True)]
    psum x1 -> x0, blocking collectives: 130 us -> none  [per_device(): lax.psum(small_sum[0].astype(jnp.bfloat16), ('ctx', 'dp'))]
    dynamic_update_slice x16 -> x0, local copies, waits for them, and re-layouts: 119 us -> none  [the longest x8 59.3 us: per_device(): lax.dynamic_update_slice_in_dim(layer_own_keys, layer_key_block[:, :, Non...]
    ppermute x64 -> x0, waiting for transfers between devices: 113 us -> none  [the longest x46 110 us: from_behind(): lax.ppermute(shard, axis, [(i, (i + by) % length) for i in range(length)])]
    ppermute x64 -> x0, starting transfers between devices: 99.2 us -> none  [the longest x18 57.2 us: passed_along(): lax.ppermute(value, axis, [(source, source + steps) for source in range(i...]
  transfers between devices with their start and end apart: 85 -> 0, of which waited for: 47 -> 0; matrix products, arithmetic and copies ran while one was open for 34% -> 0% of each run, Pallas kernels for 0% -> 0%
where the time goes in v1:
time: 477 us; the launch traced here: 476 us
  Pallas kernels  454 us (95%)
  local copies, waits for them, and re-layouts  18.2 us (4%)
    pallas_call x3, Pallas kernels, call(): pl.pallas_call(kernel, name=name, out_shape=[jax.ShapeDtypeStruct(shape,...  454 us

profile of v1, /device:TPU:0, one launch (start us, length us, event | category | flops | bytes accessed | tf_op | source)
XLA Modules:
  0.0 475.8 jit_solution(12903548351591975698)
XLA Ops:
  0.7 0.8 slice_reduce_fusion.7
  1.5 0.6 reshape.74.qo_bias
  2.3 0.6 reshape.73.kv_bias
  2.9 1.0 reshape.64
  3.9 1.0 reshape_squeeze.20
  4.9 0.3 reshape_squeeze.19
  5.2 0.2 pad_maximum_fusion.1
  5.6 1.1 convert_bitcast_fusion.shard
  6.8 66.2 %gather_weights.1.w = bf16[1280,3840]{1,0:T(8,128)(2,1)} custom-call(f32[2,40,3840]{2,1,0:T(8,128)} %convert_bitcast_fusion.shard), custom_call_target="tpu_custom_call" | custom-call | bytes 1228800 | tf_op jit(solution)/shard_map/gather_weights/pallas_call | solution.py:750
  72.9 319.7 %layers.1 = (bf16[1280,3840]{1,0:T(8,128)(2,1)}, bf16[2,64,1280]{2,1,0:T(8,128)(2,1)}, bf16[2,64,1280]{2,1,0:T(8,128)(2,1)}, f32[8,1280]{1,0:T(8,128)}, f32[8,1280]{1,0:T(8,128)}) custom-call(bf16[2,128,1280]{2,1,0:T(8,128)(2,1)} %bitcast.60, bf16[2,128,1280]{2,1,0:T(8,128)(2,1)} %bitcast.61, bf16[1280,3840]{1,0:T(8,128)(2,1)} %gather_weights.1.w, ...), custom_call_target="tpu_custom_call" | custom-call | flops 15099494400 | bytes 11192320 | tf_op jit(solution)/shard_map/layers/pallas_call | solution.py:750
  392.6 68.2 %scatter_gradients.1 = (f32[2,40,3840]{2,1,0:T(8,128)}, f32[8,1280]{1,0:T(8,128)}, f32[2,8,1280]{2,1,0:T(8,128)}, bf16[128,1280]{1,0:T(8,128)(2,1)}, bf16[128,1280]{1,0:T(8,128)(2,1)}) custom-call(bf16[1280,3840]{1,0:T(8,128)(2,1)} %get-tuple-element.21.grads, f32[8,1280]{1,0:T(8,128)} %get-tuple-element.22.home_sum, ...), custom_call_target="tpu_custom_call" | custom-call | bytes 10567680 | tf_op jit(solution)/shard_map/scatter_gradients/pallas_call | solution.py:750
  460.9 1.6 fusion.1
  462.7 0.6 maximum_bitcast_fusion
  463.3 1.5 slice_bitcast_fusion.4
  464.8 1.1 fusion
  465.9 1.2 slice_bitcast_fusion
  467.1 0.8 copy.33
  467.9 0.1 copy.28
  468.0 0.4 reshape.69
  468.4 0.1 copy.29
  468.5 0.4 reshape.70
  468.9 1.2 slice_reduce_fusion.2
  470.1 0.1 stack.13
  470.2 0.1 stack.14
  470.3 1.1 slice_reduce_fusion
  471.5 0.7 reshape_squeeze.23
  472.2 0.1 stack.12
  472.3 0.7 pad_maximum_fusion
  473.1 0.2 copy.30
  473.3 1.1 reshape.71
  474.4 0.7 copy.38
  475.1 0.7 copy.39
  (23 shorter events, 0.8 us)
Async XLA Ops:
  0.6 4.2 copy-start.2
  0.7 4.3 copy-start.3
  472.3 2.0 copy-start.1
  473.1 2.0 copy-start
